TPU v7x, 256 devices: a whole 4x4x8 slice. The times are simulated.
256 devices in a mesh: tm: 16 (over z_lo, x), rows: 16 (over z_hi, y, core).
Axes of the slice: x: 4, y: 4, z: 8 (z_hi: 2, z_lo: 4; z = z_hi * 4 + z_lo), core: 2. Of those that a mesh axis runs over, the one named last changes fastest.
Arguments:
- initial_warmth: float32 [1024, 1024], P('rows'), may hold values from -6 to 6
- pattern_choice: int32 [32, 8, 8], P('tm'), may hold values from 0 to 7
- dissipation_tables: float32 [8, 128, 128], replicated, may hold values from -6 to 6
- material_label: int32 [8, 8], replicated, may hold values from 0 to 3
- intercept_kappa: float32 [4], replicated, may hold values from 4 to 8
- sensitivity_coef: float32 [4], replicated, may hold values from -0.5 to 0.5
Outputs:
- warmth_trajectory: float32 [32, 1024, 1024], P('tm', 'rows')
All inputs are finite; a program needn't handle non-finite values.
Results may differ from a plain program's by a relative error of at most 0.0003.
Values sent between devices are 32-bit elements; how exact they have to be, the bound alone decides.
No kernel may reach another device: no remote copies, remote signals or barrier semaphores. Data moves between devices by JAX's collectives and lax.ppermute only.
A program may use at most 128 MiB of HBM per device.

v0:
```python
import functools
import math

import jax
import jax.numpy as jnp
import ml_dtypes
import numpy as np
from jax import lax
from jax.experimental import pallas as pl
from jax.experimental.pallas import tpu as pltpu
from jax.sharding import PartitionSpec as P

TILE = 128
SIZE = 1024
STEPS = 32
STRIP = 64
DEVICES = 256
ALPHA = 0.05
CROSS_WEIGHT = 1.0 / 64.0
P_BLOCK = 512
BOTH = ("tm", "rows")
F32 = jnp.float32
BF16 = jnp.bfloat16
VMEM_LIMIT = 24 * 1024 * 1024
START_LIMIT = 56 * 1024 * 1024


def halves(table):
    high = table.astype(ml_dtypes.bfloat16)
    low = (table - high.astype(np.float64)).astype(ml_dtypes.bfloat16)
    return high, low


@functools.cache
def constants():
    k = np.arange(SIZE, dtype=np.int64)
    phase = k[:, None] * (2 * k[None, :] + 1) % (4 * SIZE)
    cosines = np.cos(phase.astype(np.float64) * (math.pi / (2 * SIZE)))
    made = {}
    order = np.arange(SIZE).reshape(DEVICES, 4).T.reshape(-1)
    made["table"] = halves(cosines[order].reshape(4, DEVICES, SIZE))
    edge_rows = np.concatenate([np.arange(-1, SIZE - 1, STRIP), np.arange(STRIP, SIZE + 1, STRIP)])
    inside = (edge_rows >= 0) & (edge_rows < SIZE)
    edges = cosines.T[np.clip(edge_rows, 0, SIZE - 1)] * inside[:, None]
    made["edges"] = np.concatenate(halves(edges[:, order]), 0)
    scales = np.zeros((8, SIZE), np.float32)
    scales[0] = (2.0 - 2.0 * np.cos(np.arange(SIZE) * (math.pi / SIZE)))[order]
    scales[1] = 2.0 / SIZE
    scales[1, 0] = 1.0 / SIZE
    made["scales"] = scales
    return made


def split(values):
    high = values.astype(BF16)
    return high, (values - high.astype(F32)).astype(BF16)


def stacked(values):
    return jnp.concatenate(split(values), 0)


def dot(a, b):
    return jnp.dot(a, b, preferred_element_type=F32)


def dot_nt(a, b):
    return lax.dot_general(a, b, (((1,), (1,)), ((), ())), preferred_element_type=F32)


def rows_by_table(both, high, low, product):
    count = both.shape[0] // 2
    wide = product(both, high)
    return wide[:count] + wide[count:] + product(both[:count], low)


def table_by_rows(high, low, both):
    count = both.shape[0] // 2
    wide = dot_nt(high, both)
    return wide[:, :count] + wide[:, count:] + dot_nt(low, both[:count])


def iota(shape, dim):
    return lax.broadcasted_iota(jnp.int32, shape, dim)


def block_swap(tiles):
    shape = tiles.shape
    swapped = pltpu.roll(pltpu.roll(tiles, 4, axis=1), 64, axis=2)
    diagonal = (iota(shape, 1) < 4) == (iota(shape, 2) < 64)
    return jnp.where(diagonal, tiles, swapped)


def material_row(labels, values, ty):
    return jnp.concatenate(
        [jnp.full((1, TILE), values[labels[ty, tx]], F32) for tx in range(8)], 1
    )


def conductivity(values, base, slope):
    return base * (1.0 + slope * jnp.tanh(values))


def inner_divergence(w, k, above=None, below=None):
    shape = w.shape
    row, column = iota(shape, 0), iota(shape, 1)
    w_next = pltpu.roll(w, STRIP - 1, axis=0)
    k_next = pltpu.roll(k, STRIP - 1, axis=0)
    below = jnp.zeros((1, 1), F32) if below is None else below
    above = jnp.zeros((1, 1), F32) if above is None else above
    down = jnp.where(row == STRIP - 1, below, 0.5 * (k + k_next) * (w_next - w))
    up = jnp.where(row == 0, above, pltpu.roll(down, 1, axis=0))
    w_right = pltpu.roll(w, SIZE - 1, axis=1)
    k_right = pltpu.roll(k, SIZE - 1, axis=1)
    side = CROSS_WEIGHT * (0.5 * (k + k_right) * (w_right - w))
    side = jnp.where(column == SIZE - 1, 0.0, side)
    return down - up + (side - pltpu.roll(side, 1, axis=1))


def material_rows(labels, values, ty):
    return material_row(labels, values[0], ty), material_row(labels, values[1], ty)


def position():
    t, r = lax.axis_index("tm"), lax.axis_index("rows")
    return t, r, t * lax.axis_size("rows") + r


def start_kernel(
    labels,
    intercept,
    sensitivity,
    patterns,
    w_ref,
    table_hi,
    table_lo,
    out,
):
    t, r, _ = position()
    w = w_ref[...]
    base, slope = material_rows(labels, (intercept, sensitivity), r * STRIP // TILE)
    both = stacked(inner_divergence(w, conductivity(w, base, slope)))
    wide = dot_nt(table_hi[...], both)
    rest = dot_nt(table_lo[...], both)
    modes = wide + pltpu.roll(wide + rest, 64, axis=1)
    modes = jnp.where(iota((256, 128), 1) < 64, 0.0, modes)
    lane = iota((1, 128), 1)
    chosen = jnp.zeros((1, 128), jnp.int32)
    for tx in range(8):
        chosen = jnp.where(lane % 8 == tx, patterns[r, tx], chosen)
    one_hot = jnp.where((chosen == lane // 8) & (lane < 64), 1.0, 0.0).astype(F32)
    out[pl.ds(0, 256, stride=2), :] = modes + one_hot
    columns = pl.ds(pl.multiple_of(t // 2 * 128, 128), 128)
    first, last = w_ref[0:1, columns], w_ref[STRIP - 1 : STRIP, columns]
    first = jnp.where(t % 2 == 0, first, pltpu.roll(first, 64, axis=1))
    last = jnp.where(t % 2 == 0, pltpu.roll(last, 64, axis=1), last)
    edges = jnp.where(lane < 64, first, last)
    out[pl.ds(1, 256, stride=2), :] = jnp.broadcast_to(edges, (256, 128))


def face_fluxes(got, labels, intercept, sensitivity, own, first_ref, last_ref):
    lane = iota((16, 128), 1) < 64
    row = iota((16, 128), 0)
    totals = [jnp.zeros((16, 128), F32)] * 4
    for tx in range(8):
        columns = slice(tx * 128, tx * 128 + 128)
        left = got[tx * 32 : tx * 32 + 16]
        right = got[tx * 32 + 16 : tx * 32 + 32]
        first = jnp.where(lane, left, pltpu.roll(right, 64, axis=1))
        last = jnp.where(lane, pltpu.roll(left, 64, axis=1), right)
        first_ref[:, columns] = first
        last_ref[:, columns] = last
        base = jnp.zeros((16, 128), F32)
        slope = jnp.zeros((16, 128), F32)
        for ty in range(8):
            here = row // 2 == ty
            base = jnp.where(here, intercept[labels[ty, tx]], base)
            slope = jnp.where(here, sensitivity[labels[ty, tx]], slope)
        k_first = conductivity(first, base, slope)
        k_last = conductivity(last, base, slope)
        w_next = pltpu.roll(first, 15, axis=0)
        k_next = pltpu.roll(k_first, 15, axis=0)
        flux = jnp.where(row == 15, 0.0, 0.5 * (k_last + k_next) * (w_next - last))
        for q in range(4):
            totals[q] = totals[q] + own[q * 8 + tx : q * 8 + tx + 1, :] * flux
    sums = [jnp.sum(total, axis=1, keepdims=True) for total in totals]
    down = jnp.concatenate(sums, 0)
    up = jnp.concatenate([pltpu.roll(jnp.broadcast_to(x, (16, 128)), 1, axis=0) for x in sums], 0)
    return down, up[:, :1]


def cyclic_solve(force, rho, gain, store):
    even = iota(rho.shape, 0) < 4
    twice = 2.0 * rho
    square = rho * rho
    drives = [twice * force(tile) for tile in range(STEPS // 2)]
    pairs = [rho * pltpu.roll(drive, 4, axis=0) + drive for drive in drives]
    z = pairs[0]
    for pair in pairs[1:]:
        z = square * z + pair
    odd = gain * z
    for tile in range(STEPS // 2):
        before = rho * pltpu.roll(odd, 4, axis=0) + drives[tile]
        odd = square * odd + pairs[tile]
        store(tile, jnp.where(even, before, odd))


def make_factors(intercept, scales, device, factors):
    count = intercept.shape[0]
    conduct = intercept[0]
    for region in range(1, count):
        conduct = conduct + intercept[region]
    conduct = conduct / count
    lane = iota((1, SIZE), 1)
    row = iota((8, 128), 0) % 4
    mu = jnp.zeros((8, 128), F32)
    for q in range(4):
        chosen = jnp.where(lane == q * DEVICES + device, scales[0:1, :], 0.0)
        mu = jnp.where(row == q, jnp.sum(chosen, 1, keepdims=True), mu)
    weight = jnp.where((row == 0) & (device == 0), 1.0 / SIZE, 2.0 / SIZE)
    rho = 1.0 / (1.0 + 2.0 * (conduct * (scales[0:1, :] + CROSS_WEIGHT * mu[:, :1])))
    power = rho
    for _ in range(5):
        power = power * power
    factors[0:8, :] = rho
    factors[8:16, :] = ALPHA / (1.0 - ALPHA * power)
    factors[16:24, :] = scales[1:2, :] * weight[:, :1]


def weighted(tiles, scale):
    return stacked(jnp.concatenate([tile * scale for tile in tiles], 0))


def joined(table, first, count):
    numbers = slice(first // DEVICES, (first + count) // DEVICES)
    return table[numbers].reshape(count, SIZE)


def swap_rows(total, rows):
    for j in range(8):
        tiles = total[:, j * 128 : (j + 1) * 128].reshape(16, 8, 128)
        rows[:, j] = block_swap(tiles)


def first_solve_kernel(
    labels,
    intercept,
    sensitivity,
    received,
    tables,
    edge_table,
    scales,
    table_hi,
    table_lo,
    out,
    update,
    rest,
    near,
    factors,
    x_ref,
    rows,
    first_ref,
    last_ref,
):
    _, r, device = position()
    edges = received[pl.ds(1, 256, stride=2), :]
    group = pl.ds(pl.multiple_of(device // 16 * 16, 16), 16)
    mine = iota((16, SIZE), 0) == device % 16
    pieces = []
    for q in range(4):
        near_rows = table_hi[q, group, :].astype(F32) + table_lo[q, group, :].astype(F32)
        row = jnp.sum(jnp.where(mine, near_rows, 0.0), 0, keepdims=True)
        pieces += [row[:, tx * 128 : (tx + 1) * 128] for tx in range(8)]
    own = jnp.concatenate(pieces, 0)
    down, up = face_fluxes(edges, labels, intercept, sensitivity, own, first_ref, last_ref)
    strip = iota((16, SIZE), 0)
    near[0:1, :] = jnp.sum(jnp.where(strip == r - 1, last_ref[...], 0.0), 0, keepdims=True)
    near[1:2, :] = jnp.sum(jnp.where(strip == r + 1, first_ref[...], 0.0), 0, keepdims=True)
    near[2:8, :] = jnp.zeros((6, SIZE), F32)
    repeat = (iota((128, 32), 0) // 4 == iota((128, 32), 1)).astype(F32).astype(BF16)
    match = iota((128, 256), 0) % 4 == iota((128, 256), 1) // 64
    chosen = []
    for ty in range(8):
        part = received[pl.ds(2 * ty, 32, stride=16), :]
        part = jnp.where(iota((32, 128), 1) < 64, part, pltpu.roll(part, 64, axis=1)).astype(BF16)
        rows_nq = dot(repeat, jnp.concatenate([part, part], 1))
        chosen.append(jnp.where(match, rows_nq, 0.0).astype(BF16))
    chosen = jnp.concatenate(chosen, 0)
    by_tile = rows_by_table(stacked(own), *split(tables[...]), dot_nt)
    pieces = [
        by_tile[q * 8 : (q + 1) * 8, k * 128 : (k + 1) * 128] for q in range(4) for k in range(8)
    ]
    a_hi, a_lo = split(jnp.concatenate(pieces, 0))
    few = iota((64, 128), 1)
    inner = received[pl.ds(0, 64, stride=2), :]
    inner = inner + jnp.where(few == 127, down, 0.0) - jnp.where(few == 64, up, 0.0)
    top = jnp.where(few < 64, pltpu.roll(inner, 64, axis=1), 0.0)
    bottom = jnp.where(few < 64, 0.0, inner)
    d_hi, d_lo = split(jnp.concatenate([top, bottom], 0))
    to, source = iota((128, 128), 0), iota((128, 128), 1)
    same_mode = to % 4 == source // 16 % 4
    same_strip = source % 16 == 2 * (to // 16) + source // 64
    spread = (same_mode & same_strip).astype(F32).astype(BF16)
    power = dot(chosen, a_hi) + dot(chosen, a_lo)
    start = dot(spread, d_hi) + dot(spread, d_lo)
    for ty in range(8):
        parts = [power[ty * 128 : (ty + 1) * 128], start[ty * 16 : (ty + 1) * 16]]
        x_ref[:, ty * 128 : (ty + 1) * 128] = stacked(jnp.concatenate(parts, 0))

    make_factors(intercept, scales, device, factors)
    even = iota((8, P_BLOCK), 0) < 4
    total = jnp.zeros((128, SIZE), F32)
    edge_total = jnp.zeros((32, 128), F32)
    for block in range(SIZE // P_BLOCK):
        lanes = slice(block * P_BLOCK, (block + 1) * P_BLOCK)
        first = block * P_BLOCK
        high, low = joined(table_hi, first, P_BLOCK), joined(table_lo, first, P_BLOCK)
        modes = rows_by_table(x_ref[...], high, low, dot_nt)
        shared = modes[128:136]
        rho = factors[0:8, lanes]
        last = [jnp.zeros_like(rho)]
        tiles = []

        def force(tile):
            return modes[tile * 8 : tile * 8 + 8] + shared

        def store(tile, u):
            at = slice(tile * 8, tile * 8 + 8)
            update[at, lanes] = u
            turned = pltpu.roll(u, 4, axis=0)
            earlier = jnp.where(even, last[0], turned)
            rest[at, lanes] = modes[at] - 0.5 * (u - earlier)
            last[0] = turned
            tiles.append(u)

        cyclic_solve(force, rho, factors[8:16, lanes], store)
        u = weighted(tiles, factors[16:24, lanes])
        total = total + rows_by_table(u, high, low, dot)
        edge_total = edge_total + table_by_rows(edge_table[:32, lanes], edge_table[32:, lanes], u)

    swap_rows(total, rows)
    flat = rows.reshape(SIZE, 128)
    for q in range(4):
        out[pl.ds(q, 256, stride=5), :] = flat[pl.ds(q, 256, stride=4), :]
    low_lane = iota((16, 128), 1) < 8
    above, below = edge_total[0:16, :], edge_total[16:32, :]
    for t in range(16):
        left = pltpu.roll(above, (128 - 8 * t) % 128, axis=1)
        right = pltpu.roll(below, (136 - 8 * t) % 128, axis=1)
        out[pl.ds(80 * t + 4, 16, stride=5), :] = jnp.where(low_lane, left, right)


def second_solve_kernel(
    received, before, rest, factors, table_hi, table_lo, out, x_ref
):
    for j in range(8):
        tiles = block_swap(received[:, j])
        x_ref[:, j * 128 : (j + 1) * 128] = stacked(tiles.reshape(128, 128))
    total = jnp.zeros((128, SIZE), F32)
    for block in range(SIZE // P_BLOCK):
        lanes = slice(block * P_BLOCK, (block + 1) * P_BLOCK)
        first = block * P_BLOCK
        high, low = joined(table_hi, first, P_BLOCK), joined(table_lo, first, P_BLOCK)
        modes = rows_by_table(x_ref[...], high, low, dot_nt) + rest[:, lanes]
        rho = factors[0:8, lanes]
        tiles = []

        def force(tile):
            return modes[tile * 8 : tile * 8 + 8]

        def store(tile, u):
            tiles.append(u + before[tile * 8 : tile * 8 + 8, lanes])

        cyclic_solve(force, rho, factors[8:16, lanes], store)
        u = weighted(tiles, factors[16:24, lanes])
        total = total + rows_by_table(u, high, low, dot)
    swap_rows(total, out)


def final_kernel(received, table_hi, table_lo, initial, out):
    rows = [received[pl.ds(q, 256, stride=4), :].T for q in range(4)]
    high, low = joined(table_hi, 0, SIZE), joined(table_lo, 0, SIZE)
    update = rows_by_table(stacked(jnp.concatenate(rows, 1)), high, low, dot)
    start = initial[...]
    out[0] = update[:STRIP] + start
    out[1] = update[STRIP:] + start


def divergence_kernel(
    labels,
    intercept,
    sensitivity,
    received,
    initial,
    near,
    table_hi,
    table_lo,
    out,
    d_ref,
):
    _, r, _ = position()
    edge_rows = received[pl.ds(4, 256, stride=5), :].T[:16]
    owner = iota((16, 256), 0) % 4
    rows = []
    for q in range(4):
        inner = received[pl.ds(q, 256, stride=5), :].T
        masked = jnp.where(owner == q, edge_rows, 0.0)
        rows.append(jnp.concatenate([inner, masked], 0))
    high, low = joined(table_hi, 0, SIZE), joined(table_lo, 0, SIZE)
    update = rows_by_table(stacked(jnp.concatenate(rows, 1)), high, low, dot)
    values = (intercept, sensitivity)
    first = r * STRIP
    own = material_rows(labels, values, first // TILE)
    above = material_rows(labels, values, jnp.maximum(first - 1, 0) // TILE)
    below = material_rows(labels, values, jnp.minimum(first + STRIP, SIZE - 1) // TILE)
    start = initial[...]
    for n in range(2):
        w = update[n * STRIP : (n + 1) * STRIP] + start
        k = conductivity(w, *own)
        at = 128 + 4 * n
        w_above = near[0:1, :] + jnp.sum(update[at : at + 4], 0, keepdims=True)
        w_below = near[1:2, :] + jnp.sum(update[at + 8 : at + 12], 0, keepdims=True)
        k_above = conductivity(w_above, *above)
        k_below = conductivity(w_below, *below)
        enter = 0.5 * (k_above + k[:1]) * (w[:1] - w_above)
        leave = 0.5 * (k_below + k[STRIP - 1 :]) * (w_below - w[STRIP - 1 :])
        enter = jnp.where(r == 0, 0.0, enter)
        leave = jnp.where(r == SIZE // STRIP - 1, 0.0, leave)
        d_ref[n * STRIP : (n + 1) * STRIP, :] = inner_divergence(w, k, enter, leave)
    d = stacked(d_ref[...])
    for q in range(4):
        out[pl.ds(q, 256, stride=4), :] = table_by_rows(table_hi[q], table_lo[q], d)


def whole(shape):
    return pl.BlockSpec(shape, lambda i: (0,) * len(shape))


SMEM = pl.BlockSpec(memory_space=pltpu.SMEM)


def call(kernel, limit, in_specs, outs, scratch, *args):
    results = pl.pallas_call(
        kernel,
        grid=(1,),
        in_specs=in_specs,
        out_specs=[whole(out) for out in outs],
        scratch_shapes=scratch,
        out_shape=[jax.ShapeDtypeStruct(out, F32) for out in outs],
        compiler_params=pltpu.CompilerParams(vmem_limit_bytes=limit),
    )(*args)
    return results if len(outs) > 1 else results[0]


def exchange(tiles, width):
    shape = (DEVICES, width // 128, 128) if width in (256, 512) else (DEVICES, 1, width)
    moved = lax.all_to_all(tiles.reshape(shape), BOTH, split_axis=0, concat_axis=0, tiled=True)
    return moved.reshape(-1, 128)


def shards(
    initial_warmth,
    pattern_choice,
    dissipation_tables,
    material_label,
    intercept_kappa,
    sensitivity_coef,
):
    made = constants()
    material = (material_label, intercept_kappa, sensitivity_coef)
    table = made["table"]
    one_number = pl.BlockSpec((None, 256, SIZE), lambda i: (lax.rem(lax.axis_index("tm"), 4), 0, 0))
    tables = [whole((4, 256, SIZE))] * 2
    strip = whole((STRIP, SIZE))
    field = whole((128, SIZE))
    few = whole((8, SIZE))
    sent = call(
        start_kernel,
        START_LIMIT,
        [SMEM] * 4 + [strip, one_number, one_number],
        [(512, 128)],
        [],
        *material,
        pattern_choice.reshape(16, 8),
        initial_warmth,
        *table,
    )
    received = exchange(sent, 256)
    sent, before, rest, near, factors = call(
        first_solve_kernel,
        VMEM_LIMIT,
        [SMEM] * 3
        + [
            whole((512, 128)),
            whole((SIZE, 128)),
            whole((64, SIZE)),
            few,
            *tables,
        ],
        [(1280, 128), (128, SIZE), (128, SIZE), (8, SIZE), (24, SIZE)],
        [
            pltpu.VMEM((288, SIZE), BF16),
            pltpu.VMEM((16, 8, 8, 128), F32),
            pltpu.VMEM((16, SIZE), F32),
            pltpu.VMEM((16, SIZE), F32),
        ],
        *material,
        received,
        dissipation_tables.reshape(SIZE, 128),
        made["edges"],
        made["scales"],
        *table,
    )
    received = exchange(sent, 640)
    sent = call(
        divergence_kernel,
        VMEM_LIMIT,
        [SMEM] * 3 + [whole((1280, 128)), strip, few, *tables],
        [(SIZE, 128)],
        [pltpu.VMEM((128, SIZE), F32)],
        *material,
        received,
        initial_warmth,
        near,
        *table,
    )
    received = exchange(sent, 512)
    sent = call(
        second_solve_kernel,
        VMEM_LIMIT,
        [whole((16, 8, 8, 128)), field, field, whole((24, SIZE)), *tables],
        [(16, 8, 8, 128)],
        [pltpu.VMEM((256, SIZE), BF16)],
        received.reshape(16, 8, 8, 128),
        before,
        rest,
        factors,
        *table,
    )
    received = exchange(sent, 512)
    return call(
        final_kernel,
        VMEM_LIMIT,
        [whole((SIZE, 128)), *tables, strip],
        [(2, STRIP, SIZE)],
        [],
        received,
        *table,
        initial_warmth,
    )


def solution(mesh):
    in_specs = (P("rows", None), P("tm", None, None), P(), P(), P(), P())
    out_specs = P("tm", "rows", None)
    return jax.shard_map(shards, mesh=mesh, in_specs=in_specs, out_specs=out_specs, check_vma=False)
```

profile of v0, /device:TPU:1, one launch (start us, length us, event | category | flops | bytes accessed | tf_op | source)
XLA Modules:
  0.0 128.7 jit_solution(16206745666485589037)
XLA Ops:
  0.0 0.0 copy-start
  0.0 0.0 copy-start.1
  0.0 0.0 copy-start.3
  0.0 0.0 copy-start.4
  0.0 0.0 copy-start.5
  0.0 0.0 copy-start.6
  0.0 0.0 copy-start.7
  0.1 0.0 copy-start.8
  0.1 3.0 %shard_map.100 = f32[512,128]{1,0:T(8,128)} custom-call(s32[8,8]{1,0:T(8,128)} %labels.5, f32[4]{0:T(128)} %intercept.5, f32[4]{0:T(128)} %sensitivity.5, s32[16,8]{1,0:T(8,128)} %bitcast.19, f32[64,1024]{1,0:T(8,128)} %initial.3, bf16[4,256,1024]{2,1,0:T(8,128)(2,1)} %constant.8.clone.table_hi, bf16[4,256,1024]{2,1,0:T(8,128)(2,1)} %constant.9.clone.table_lo), custom_call_target="tpu_custom_call" | custom-call | tf_op jit(solution)/shard_map/pallas_call | solution.py:443
  3.1 31.2 %all_to_all.20 = f32[256,2,128]{2,1,0:T(2,128)S(1)} all-to-all(f32[256,2,128]{2,1,0:T(2,128)} %bitcast.18), channel_id=1, replica_groups=mesh['tm'=16,'rows'=16] {'tm','rows'}, dimensions={0} | all-to-all | bytes 524288 | tf_op jit(solution)/shard_map/all_to_all | solution.py:457
  34.3 0.0 copy-done
  34.3 0.0 copy-done.1
  34.3 0.0 copy-done.3
  34.3 0.0 copy-done.4
  34.3 0.0 copy-done.5
  34.4 0.0 copy-done.6
  34.4 0.0 copy-done.7
  34.4 0.0 copy-done.8
  34.4 0.0 copy-start.2
  34.4 5.6 %shard_map.101 = (f32[1280,128]{1,0:T(8,128)S(1)}, f32[128,1024]{1,0:T(8,128)S(1)}, f32[128,1024]{1,0:T(8,128)S(1)}, f32[8,1024]{1,0:T(8,128)S(1)}, f32[24,1024]{1,0:T(8,128)S(1)}) custom-call(s32[8,8]{1,0:T(8,128)S(1)} %copy-done.5, f32[4]{0:T(128)S(1)} %copy-done.7, f32[4]{0:T(128)S(1)} %copy-done.8, f32[512,128]{1,0:T(8,128)S(1)} %bitcast.15, ...), custom_call_target="tpu_custom_call" | custom-call | tf_op jit(solution)/shard_map/pallas_call | solution.py:443
  40.0 28.9 %all_to_all.21 = f32[256,1,640]{2,1,0:T(1,128)S(1)} all-to-all(f32[256,1,640]{2,1,0:T(1,128)S(1)} %bitcast.16), channel_id=1, replica_groups=mesh['tm'=16,'rows'=16] {'tm','rows'}, dimensions={0} | all-to-all | bytes 1310720 | tf_op jit(solution)/shard_map/all_to_all | solution.py:457
  68.9 0.0 copy-done.2
  68.9 3.4 %shard_map.102 = f32[1024,128]{1,0:T(8,128)S(1)} custom-call(s32[8,8]{1,0:T(8,128)S(1)} %copy-done.5, f32[4]{0:T(128)S(1)} %copy-done.7, f32[4]{0:T(128)S(1)} %copy-done.8, f32[1280,128]{1,0:T(8,128)S(1)} %bitcast.10, f32[64,1024]{1,0:T(8,128)S(1)} %copy-done.2, f32[8,1024]{1,0:T(8,128)S(1)} %get-tuple-element.11.near, bf16[4,256,1024]{2,1,0:T(8,128)(2,1)S(1)} %copy-done.1, ...), custom_call_target="tpu_custom_call" | custom-call | tf_op jit(solution)/shard_map/pallas_call | solution.py:443
  72.3 26.0 %all_to_all.22 = f32[256,4,128]{2,1,0:T(4,128)S(1)} all-to-all(f32[256,4,128]{2,1,0:T(4,128)S(1)} %bitcast.14), channel_id=1, replica_groups=mesh['tm'=16,'rows'=16] {'tm','rows'}, dimensions={0} | all-to-all | bytes 1048576 | tf_op jit(solution)/shard_map/all_to_all | solution.py:457
  98.3 2.7 %shard_map.103 = f32[16,8,8,128]{3,2,1,0:T(8,128)S(1)} custom-call(f32[16,8,8,128]{3,2,1,0:T(8,128)S(1)} %bitcast.11, f32[128,1024]{1,0:T(8,128)S(1)} %get-tuple-element.12.before, f32[128,1024]{1,0:T(8,128)S(1)} %get-tuple-element.13.rest, f32[24,1024]{1,0:T(8,128)S(1)} %get-tuple-element.14.factors, bf16[4,256,1024]{2,1,0:T(8,128)(2,1)S(1)} %copy-done.1, ...), custom_call_target="tpu_custom_call" | custom-call | tf_op jit(solution)/shard_map/pallas_call | solution.py:443
  101.0 25.8 %all_to_all.23 = f32[256,4,128]{2,1,0:T(4,128)S(1)} all-to-all(f32[256,4,128]{2,1,0:T(4,128)S(1)} %bitcast.12), channel_id=1, replica_groups=mesh['tm'=16,'rows'=16] {'tm','rows'}, dimensions={0} | all-to-all | bytes 1048576 | tf_op jit(solution)/shard_map/all_to_all | solution.py:457
  126.9 1.8 %shard_map.104 = f32[2,64,1024]{2,1,0:T(8,128)} custom-call(f32[1024,128]{1,0:T(8,128)S(1)} %bitcast.13, bf16[4,256,1024]{2,1,0:T(8,128)(2,1)S(1)} %copy-done.1, bf16[4,256,1024]{2,1,0:T(8,128)(2,1)S(1)} %copy-done, f32[64,1024]{1,0:T(8,128)S(1)} %copy-done.2), custom_call_target="tpu_custom_call" | custom-call | tf_op jit(solution)/shard_map/pallas_call | solution.py:443
Async XLA Ops:
  0.0 34.3 %copy-start = (bf16[4,256,1024]{2,1,0:T(8,128)(2,1)S(1)}, bf16[4,256,1024]{2,1,0:T(8,128)(2,1)}, u32[]{:S(2)}) copy-start(bf16[4,256,1024]{2,1,0:T(8,128)(2,1)} %constant.9.clone.table_lo) | copy-start | bytes 6291460
  0.0 34.3 %copy-start.1 = (bf16[4,256,1024]{2,1,0:T(8,128)(2,1)S(1)}, bf16[4,256,1024]{2,1,0:T(8,128)(2,1)}, u32[]{:S(2)}) copy-start(bf16[4,256,1024]{2,1,0:T(8,128)(2,1)} %constant.8.clone.table_hi) | copy-start | bytes 6291460
  0.0 34.3 %copy-start.3 = (f32[8,128,128]{2,1,0:T(8,128)S(1)}, f32[8,128,128]{2,1,0:T(8,128)}, u32[]{:S(2)}) copy-start(f32[8,128,128]{2,1,0:T(8,128)} %param.12) | copy-start | bytes 1572868
  0.0 34.3 %copy-start.4 = (bf16[64,1024]{1,0:T(8,128)(2,1)S(1)}, bf16[64,1024]{1,0:T(8,128)(2,1)}, u32[]{:S(2)}) copy-start(bf16[64,1024]{1,0:T(8,128)(2,1)} %constant.10.clone.edge_table) | copy-start | bytes 393220
  0.0 34.3 %copy-start.5 = (s32[8,8]{1,0:T(8,128)S(1)}, s32[8,8]{1,0:T(8,128)}, u32[]{:S(2)}) copy-start(s32[8,8]{1,0:T(8,128)} %labels.5) | copy-start | bytes 772
  0.0 34.3 %copy-start.6 = (f32[8,1024]{1,0:T(8,128)S(1)}, f32[8,1024]{1,0:T(8,128)}, u32[]{:S(2)}) copy-start(f32[8,1024]{1,0:T(8,128)} %constant.11.clone.scales) | copy-start | bytes 98308
  0.0 34.3 %copy-start.7 = (f32[4]{0:T(128)S(1)}, f32[4]{0:T(128)}, u32[]{:S(2)}) copy-start(f32[4]{0:T(128)} %intercept.5) | copy-start | bytes 52
  0.1 34.3 %copy-start.8 = (f32[4]{0:T(128)S(1)}, f32[4]{0:T(128)}, u32[]{:S(2)}) copy-start(f32[4]{0:T(128)} %sensitivity.5) | copy-start | bytes 52
  34.4 34.5 %copy-start.2 = (f32[64,1024]{1,0:T(8,128)S(1)}, f32[64,1024]{1,0:T(8,128)}, u32[]{:S(2)}) copy-start(f32[64,1024]{1,0:T(8,128)} %initial.3) | copy-start | bytes 786436
where the time goes:
time: 129 us
  blocking collectives  112 us (87%)
  Pallas kernels  16.6 us (13%)
    all_to_all x4, blocking collectives, exchange(): lax.all_to_all(tiles.reshape(shape), BOTH, split_axis=0, concat_axis=0, t...  112 us
    pallas_call x5, Pallas kernels, call(): pl.pallas_call(kernel, grid=(1,), in_specs=in_specs, out_specs=[whole(out...  16.6 us

commit v1 on v0

--- a/solution.py
+++ b/solution.py
@@ -17,7 +17,7 @@
 DEVICES = 256
 ALPHA = 0.05
 CROSS_WEIGHT = 1.0 / 64.0
-P_BLOCK = 512
+P_BLOCK = 1024
 BOTH = ("tm", "rows")
 F32 = jnp.float32
 BF16 = jnp.bfloat16

time: 129 us -> 128 us (level)
  no operation moved by 1% of the time
where the time goes in v1:
time: 128 us
  blocking collectives  112 us (88%)
  Pallas kernels  15.7 us (12%)
    all_to_all x4, blocking collectives, exchange(): lax.all_to_all(tiles.reshape(shape), BOTH, split_axis=0, concat_axis=0, t...  112 us
    pallas_call x5, Pallas kernels, call(): pl.pallas_call(kernel, grid=(1,), in_specs=in_specs, out_specs=[whole(out...  15.7 us

profile of v1, /device:TPU:1, one launch (start us, length us, event | category | flops | bytes accessed | tf_op | source)
XLA Modules:
  0.0 127.8 jit_solution(10451756899001344673)
XLA Ops:
  0.0 0.0 copy-start
  0.0 0.0 copy-start.1
  0.0 0.0 copy-start.3
  0.0 0.0 copy-start.4
  0.0 0.0 copy-start.5
  0.0 0.0 copy-start.6
  0.0 0.0 copy-start.7
  0.1 0.0 copy-start.8
  0.1 3.0 %shard_map.100 = f32[512,128]{1,0:T(8,128)} custom-call(s32[8,8]{1,0:T(8,128)} %labels.5, f32[4]{0:T(128)} %intercept.5, f32[4]{0:T(128)} %sensitivity.5, s32[16,8]{1,0:T(8,128)} %bitcast.19, f32[64,1024]{1,0:T(8,128)} %initial.3, bf16[4,256,1024]{2,1,0:T(8,128)(2,1)} %constant.8.clone.table_hi, bf16[4,256,1024]{2,1,0:T(8,128)(2,1)} %constant.9.clone.table_lo), custom_call_target="tpu_custom_call" | custom-call | tf_op jit(solution)/shard_map/pallas_call | solution.py:443
  3.1 31.2 %all_to_all.20 = f32[256,2,128]{2,1,0:T(2,128)S(1)} all-to-all(f32[256,2,128]{2,1,0:T(2,128)} %bitcast.18), channel_id=1, replica_groups=mesh['tm'=16,'rows'=16] {'tm','rows'}, dimensions={0} | all-to-all | bytes 524288 | tf_op jit(solution)/shard_map/all_to_all | solution.py:457
  34.3 0.0 copy-done
  34.3 0.0 copy-done.1
  34.3 0.0 copy-done.3
  34.3 0.0 copy-done.4
  34.3 0.0 copy-done.5
  34.4 0.0 copy-done.6
  34.4 0.0 copy-done.7
  34.4 0.0 copy-done.8
  34.4 0.0 copy-start.2
  34.4 5.0 %shard_map.101 = (f32[1280,128]{1,0:T(8,128)S(1)}, f32[128,1024]{1,0:T(8,128)S(1)}, f32[128,1024]{1,0:T(8,128)S(1)}, f32[8,1024]{1,0:T(8,128)S(1)}, f32[24,1024]{1,0:T(8,128)S(1)}) custom-call(s32[8,8]{1,0:T(8,128)S(1)} %copy-done.5, f32[4]{0:T(128)S(1)} %copy-done.7, f32[4]{0:T(128)S(1)} %copy-done.8, f32[512,128]{1,0:T(8,128)S(1)} %bitcast.15, ...), custom_call_target="tpu_custom_call" | custom-call | tf_op jit(solution)/shard_map/pallas_call | solution.py:443
  39.4 28.9 %all_to_all.21 = f32[256,1,640]{2,1,0:T(1,128)S(1)} all-to-all(f32[256,1,640]{2,1,0:T(1,128)S(1)} %bitcast.16), channel_id=1, replica_groups=mesh['tm'=16,'rows'=16] {'tm','rows'}, dimensions={0} | all-to-all | bytes 1310720 | tf_op jit(solution)/shard_map/all_to_all | solution.py:457
  68.3 0.0 copy-done.2
  68.3 3.4 %shard_map.102 = f32[1024,128]{1,0:T(8,128)S(1)} custom-call(s32[8,8]{1,0:T(8,128)S(1)} %copy-done.5, f32[4]{0:T(128)S(1)} %copy-done.7, f32[4]{0:T(128)S(1)} %copy-done.8, f32[1280,128]{1,0:T(8,128)S(1)} %bitcast.10, f32[64,1024]{1,0:T(8,128)S(1)} %copy-done.2, f32[8,1024]{1,0:T(8,128)S(1)} %get-tuple-element.11.near, bf16[4,256,1024]{2,1,0:T(8,128)(2,1)S(1)} %copy-done.1, ...), custom_call_target="tpu_custom_call" | custom-call | tf_op jit(solution)/shard_map/pallas_call | solution.py:443
  71.7 26.0 %all_to_all.22 = f32[256,4,128]{2,1,0:T(4,128)S(1)} all-to-all(f32[256,4,128]{2,1,0:T(4,128)S(1)} %bitcast.14), channel_id=1, replica_groups=mesh['tm'=16,'rows'=16] {'tm','rows'}, dimensions={0} | all-to-all | bytes 1048576 | tf_op jit(solution)/shard_map/all_to_all | solution.py:457
  97.7 2.5 %shard_map.103 = f32[16,8,8,128]{3,2,1,0:T(8,128)S(1)} custom-call(f32[16,8,8,128]{3,2,1,0:T(8,128)S(1)} %bitcast.11, f32[128,1024]{1,0:T(8,128)S(1)} %get-tuple-element.12.before, f32[128,1024]{1,0:T(8,128)S(1)} %get-tuple-element.13.rest, f32[24,1024]{1,0:T(8,128)S(1)} %get-tuple-element.14.factors, bf16[4,256,1024]{2,1,0:T(8,128)(2,1)S(1)} %copy-done.1, ...), custom_call_target="tpu_custom_call" | custom-call | tf_op jit(solution)/shard_map/pallas_call | solution.py:443
  100.2 25.8 %all_to_all.23 = f32[256,4,128]{2,1,0:T(4,128)S(1)} all-to-all(f32[256,4,128]{2,1,0:T(4,128)S(1)} %bitcast.12), channel_id=1, replica_groups=mesh['tm'=16,'rows'=16] {'tm','rows'}, dimensions={0} | all-to-all | bytes 1048576 | tf_op jit(solution)/shard_map/all_to_all | solution.py:457
  126.0 1.8 %shard_map.104 = f32[2,64,1024]{2,1,0:T(8,128)} custom-call(f32[1024,128]{1,0:T(8,128)S(1)} %bitcast.13, bf16[4,256,1024]{2,1,0:T(8,128)(2,1)S(1)} %copy-done.1, bf16[4,256,1024]{2,1,0:T(8,128)(2,1)S(1)} %copy-done, f32[64,1024]{1,0:T(8,128)S(1)} %copy-done.2), custom_call_target="tpu_custom_call" | custom-call | tf_op jit(solution)/shard_map/pallas_call | solution.py:443
Async XLA Ops:
  0.0 34.3 %copy-start = (bf16[4,256,1024]{2,1,0:T(8,128)(2,1)S(1)}, bf16[4,256,1024]{2,1,0:T(8,128)(2,1)}, u32[]{:S(2)}) copy-start(bf16[4,256,1024]{2,1,0:T(8,128)(2,1)} %constant.9.clone.table_lo) | copy-start | bytes 6291460
  0.0 34.3 %copy-start.1 = (bf16[4,256,1024]{2,1,0:T(8,128)(2,1)S(1)}, bf16[4,256,1024]{2,1,0:T(8,128)(2,1)}, u32[]{:S(2)}) copy-start(bf16[4,256,1024]{2,1,0:T(8,128)(2,1)} %constant.8.clone.table_hi) | copy-start | bytes 6291460
  0.0 34.3 %copy-start.3 = (f32[8,128,128]{2,1,0:T(8,128)S(1)}, f32[8,128,128]{2,1,0:T(8,128)}, u32[]{:S(2)}) copy-start(f32[8,128,128]{2,1,0:T(8,128)} %param.12) | copy-start | bytes 1572868
  0.0 34.3 %copy-start.4 = (bf16[64,1024]{1,0:T(8,128)(2,1)S(1)}, bf16[64,1024]{1,0:T(8,128)(2,1)}, u32[]{:S(2)}) copy-start(bf16[64,1024]{1,0:T(8,128)(2,1)} %constant.10.clone.edge_table) | copy-start | bytes 393220
  0.0 34.3 %copy-start.5 = (s32[8,8]{1,0:T(8,128)S(1)}, s32[8,8]{1,0:T(8,128)}, u32[]{:S(2)}) copy-start(s32[8,8]{1,0:T(8,128)} %labels.5) | copy-start | bytes 772
  0.0 34.3 %copy-start.6 = (f32[8,1024]{1,0:T(8,128)S(1)}, f32[8,1024]{1,0:T(8,128)}, u32[]{:S(2)}) copy-start(f32[8,1024]{1,0:T(8,128)} %constant.11.clone.scales) | copy-start | bytes 98308
  0.0 34.3 %copy-start.7 = (f32[4]{0:T(128)S(1)}, f32[4]{0:T(128)}, u32[]{:S(2)}) copy-start(f32[4]{0:T(128)} %intercept.5) | copy-start | bytes 52
  0.1 34.3 %copy-start.8 = (f32[4]{0:T(128)S(1)}, f32[4]{0:T(128)}, u32[]{:S(2)}) copy-start(f32[4]{0:T(128)} %sensitivity.5) | copy-start | bytes 52
  34.4 33.9 %copy-start.2 = (f32[64,1024]{1,0:T(8,128)S(1)}, f32[64,1024]{1,0:T(8,128)}, u32[]{:S(2)}) copy-start(f32[64,1024]{1,0:T(8,128)} %initial.3) | copy-start | bytes 786436
